TPU v7x, 256 devices: a whole 4x4x8 slice. The times are simulated.
256 devices in a mesh: dp: 16 (over y, x), opt: 16 (over z, core).
Axes of the slice: x: 4, y: 4, z: 8, core: 2. Of those that a mesh axis runs over, the one named last changes fastest.
Arguments:
- inputs: bfloat16 [2, 8192, 4096], P(None, 'dp'), may hold values from -6 to 6
- output_grads: bfloat16 [8192, 16384], P('dp', 'opt'), may hold values from -0.0625 to 0.0625
- owner_map: int32 [16, 16], P('dp'), may hold values from 0 to 15, as said below
- left_stats: bfloat16 [16, 16, 2, 512, 512], P('dp', 'opt'), may hold values from -10 to 40, as said below
- right_stats: bfloat16 [16, 16, 2, 512, 512], P('dp', 'opt'), may hold values from -10 to 40, as said below
- left_roots: bfloat16 [16, 16, 2, 512, 512], P('dp', 'opt'), may hold values from -4 to 10, as said below
- right_roots: bfloat16 [16, 16, 2, 512, 512], P('dp', 'opt'), may hold values from -4 to 10, as said below
Outputs:
- update: bfloat16 [16, 16, 512, 512], P('opt', 'dp')
- left_updated: bfloat16 [16, 16, 2, 512, 512], P('dp', 'opt')
- right_updated: bfloat16 [16, 16, 2, 512, 512], P('dp', 'opt')
Inputs may be any that keep to these rules, and one draw needn't show every extreme that they name: `owner_map`: in every row each owner is named at most 2 times, and 4 owners are named exactly 2 times. `left_stats`: each block is symmetric. `right_stats`: each block is symmetric. `left_roots`: each block is symmetric. `right_roots`: each block is symmetric.
All inputs are finite; a program needn't handle non-finite values.
Results may differ from a plain program's by a relative error of at most 0.023.
Values may be sent and summed in bfloat16 or wider, within the bound.
No kernel may reach another device: no remote copies, remote signals or barrier semaphores. Data moves between devices by JAX's collectives and lax.ppermute only.
A program may use at most 128 MiB of HBM per device.

v0:
```python
import functools

import jax
import jax.numpy as jnp
from jax import lax
from jax.experimental import pallas as pl
from jax.experimental.pallas import tpu as pltpu
from jax.sharding import PartitionSpec as P

DECAY_RATE = 0.95
SIDE = 4
OFF = [(i, j) for i in range(4) for j in range(i + 1, 4)]
VMEM_BYTES = 20 * 1024 * 1024
WEIGHT = 100
EXTRA = 16
F32 = jnp.float32
BF16 = jnp.bfloat16


def params(limit=VMEM_BYTES):
    return pltpu.CompilerParams(vmem_limit_bytes=limit)


def cost(flops, moved):
    return pl.CostEstimate(flops=int(flops), bytes_accessed=int(moved), transcendentals=0)


def x_ring(step):
    return [(y * SIDE + x, y * SIDE + (x + step) % SIDE) for y in range(SIDE) for x in range(SIDE)]


def y_ring(step):
    return [(y * SIDE + x, ((y + step) % SIDE) * SIDE + x) for y in range(SIDE) for x in range(SIDE)]


def dot(a, b, over_a, over_b):
    return lax.dot_general(a, b, (((over_a,), (over_b,)), ((), ())), preferred_element_type=F32)


def partial_kernel(steps, place, source, target, *refs):
    count = 2 * len(steps)
    extra = (len(refs) - 5 - 2 * count) // 2
    terms, results = refs[:extra], refs[extra : extra + count]
    held, outs = refs[extra + count : 2 * extra + count], refs[2 * extra + count : -5]
    rows, cols, sems, out_sems, term_sems = refs[-5:]
    block = cols.shape[1] // 2
    half = block // 2
    chooser, y, x = place[0], place[1], place[2]

    def units_of(r, along_x):
        for t in range(SIDE):
            k_y = lax.rem(y + (t if along_x else r), SIDE)
            k_x = lax.rem(x + (r if along_x else t), SIDE)
            row = (2 * k_y + lax.div(k_x, 2)) * block + (0 if along_x else half)
            yield t, pl.multiple_of(row, half), pl.multiple_of(lax.rem(k_x, 2) * block, block)

    def load(i, row):
        at = pl.ds(row, half)
        return pltpu.make_async_copy(source.at[chooser, :, at], rows.at[:, at], sems.at[i])

    plan = []
    for r in steps:
        side = lax.div(lax.rem(x + r, SIDE), 2)
        plan += [(2 * lax.rem(y + t, SIDE) + side) * block for t in range(SIDE)]
    upper = len(plan)
    for r in steps:
        plan += [(2 * lax.rem(y + r, SIDE) + side) * block + half for side in range(2)]
    copies = [load(i, pl.multiple_of(row, half)) for i, row in enumerate(plan)]
    side = lax.rem(x + steps[0], 2)
    halves = []
    for i in range(2):
        at = pl.ds(pl.multiple_of(lax.rem(side + i, 2) * block, block), block)
        halves.append(pltpu.make_async_copy(target.at[:, at], cols.at[:, at], sems.at[len(plan) + i]))
    halves[0].start()
    for copy in copies[:SIDE]:
        copy.start()
    halves[1].start()
    for copy in copies[SIDE:]:
        copy.start()
    fetched = [pltpu.make_async_copy(term, held[o], term_sems.at[o]) for o, term in enumerate(terms)]
    for copy in fetched:
        copy.start()
    halves[0].wait()
    waited = [0]

    def wait_to(n):
        for copy in copies[waited[0] : n]:
            copy.wait()
        waited[0] = max(waited[0], n)

    leaving = []
    for along_x in (True, False):
        if not along_x:
            halves[1].wait()
        for n, r in enumerate(steps):
            o = 2 * n + (0 if along_x else 1)
            for i, (t, row, col) in enumerate(units_of(r, along_x)):
                if along_x:
                    wait_to(SIDE * n + i + 1)
                else:
                    wait_to(upper + 2 * (n + 1))
                value = dot(rows[:, pl.ds(row, half)], cols[:, pl.ds(col, block)], 0, 0)
                if terms:
                    if t == 0:
                        fetched[o].wait()
                    value = value + held[o][t].astype(F32)
                outs[o][t] = value.astype(BF16)
            leaving.append(pltpu.make_async_copy(outs[o], results[o], out_sems.at[o]))
            leaving[-1].start()
    wait_to(len(plan))
    for copy in leaving:
        copy.wait()


def partials(inputs, output_grads, place, steps, block, terms=(), weight=1):
    tok, feats = inputs.shape[1:]
    half = block // 2
    count = 2 * len(steps)
    units = SIDE * count
    shape = (SIDE, half, block)
    hbm = pl.BlockSpec(memory_space=pltpu.HBM)
    return pl.pallas_call(
        functools.partial(partial_kernel, steps),
        in_specs=[pl.BlockSpec(memory_space=pltpu.SMEM)] + [hbm] * (2 + len(terms)),
        out_specs=[hbm] * count,
        out_shape=[pltpu.HBM(shape, BF16)] * count,
        scratch_shapes=[pltpu.VMEM(shape, BF16)] * (len(terms) + count)
        + [
            pltpu.VMEM((tok, feats), BF16),
            pltpu.VMEM(output_grads.shape, BF16),
            pltpu.SemaphoreType.DMA((4 * SIDE + 2,)),
            pltpu.SemaphoreType.DMA((count,)),
            pltpu.SemaphoreType.DMA((2,)),
        ],
        compiler_params=params(),
        cost_estimate=cost(
            2 * units * tok * half * block * weight,
            2 * (tok * feats + output_grads.size + units * half * block),
        ),
        name="partials",
    )(place, *[pltpu.with_memory_space_constraint(a, pltpu.HBM) for a in (inputs, output_grads, *terms)])


def grid_masks(n):
    rows = lax.broadcasted_iota(jnp.int32, (n, n), 0)
    cols = lax.broadcasted_iota(jnp.int32, (n, n), 1)
    return rows, cols


def pack_kernel(left, right, out):
    q = left.shape[-1] // 4
    parts = out.shape[0]
    per = parts // 8
    step = q // per
    rows, cols = grid_masks(q)

    def put(slot, piece, value):
        for h in range(per):
            out[piece * per + h, slot * step : (slot + 1) * step] = value[h * step : (h + 1) * step]

    lines = []
    for c in range(left.shape[0]):
        for m, ref in enumerate((left, right)):

            def quarter(i, j, ref=ref, c=c):
                return ref[c, i * q : (i + 1) * q, j * q : (j + 1) * q]

            for n, (i, j) in enumerate(OFF):
                put(2 * c + m, n, quarter(i, j))
            for h in range(2):
                upper, lower = quarter(2 * h, 2 * h), quarter(2 * h + 1, 2 * h + 1)
                put(2 * c + m, len(OFF) + h, jnp.where(rows <= cols, upper, lower))
                lines.append(jnp.sum(jnp.where(rows == cols, lower.astype(F32), 0.0), axis=0, keepdims=True))
    lines.append(jnp.zeros((EXTRA - len(lines), q), F32))
    extra = jnp.concatenate(lines, axis=0).astype(BF16)
    for j in range(parts):
        out[j, 2 * left.shape[0] * step :] = extra


def pack_roots(left, right, parts):
    cap, block = left.shape[0], left.shape[-1]
    q = block // 4
    shape = (parts, 2 * cap * (8 * q // parts) + EXTRA, q)
    return pl.pallas_call(
        pack_kernel,
        out_shape=jax.ShapeDtypeStruct(shape, BF16),
        compiler_params=params(),
        cost_estimate=cost(0, 3 * 2 * left.size),
        name="pack_roots",
    )(left, right)


def pick_roots_kernel(slots, src, out):
    body = out.shape[1] - EXTRA
    cap = (src.shape[1] - EXTRA) // body
    for i in range(out.shape[0]):
        owner, rank = lax.div(slots[i], cap), lax.rem(slots[i], cap)
        out[i, :body] = src[owner, pl.ds(pl.multiple_of(rank * body, body), body)]
        out[i, body:] = src[owner, cap * body :]


def pick_roots(slots, src, cap):
    rows = (src.shape[1] - EXTRA) // cap + EXTRA
    return pl.pallas_call(
        pick_roots_kernel,
        in_specs=[pl.BlockSpec(memory_space=pltpu.SMEM), pl.BlockSpec(memory_space=pltpu.VMEM)],
        out_specs=pl.BlockSpec(memory_space=pltpu.VMEM),
        out_shape=jax.ShapeDtypeStruct((slots.shape[0], rows, src.shape[2]), src.dtype),
        compiler_params=params(),
        cost_estimate=cost(0, 4 * src.size),
        name="pick_roots",
    )(slots, src)


def pick_kernel(index, src, out):
    for i in range(out.shape[0]):
        at = index[i]

        @pl.when(at >= 0)
        def _(i=i, at=at):
            out[i] = src[jnp.maximum(at, 0)]

        @pl.when(at < 0)
        def _(i=i):
            out[i] = jnp.zeros(out.shape[1:], out.dtype)


def pick(index, src):
    shape = (index.shape[0],) + src.shape[1:]
    return pl.pallas_call(
        pick_kernel,
        in_specs=[pl.BlockSpec(memory_space=pltpu.SMEM), pl.BlockSpec(memory_space=pltpu.VMEM)],
        out_specs=pl.BlockSpec(memory_space=pltpu.VMEM),
        out_shape=jax.ShapeDtypeStruct(shape, src.dtype),
        compiler_params=params(),
        cost_estimate=cost(0, 4 * src.size),
        name="pick",
    )(index, src)


def unpack_kernel(ranks, packed, out):
    q = out.shape[-1] // 4
    per = packed.shape[0] // 8
    step = q // per
    rows, cols = grid_masks(q)
    rank = ranks[0]
    lines = packed[0, 2 * step :].astype(F32)
    for m in range(2):

        def piece(n, m=m):
            return jnp.concatenate([packed[n * per + h, m * step : (m + 1) * step] for h in range(per)], axis=0)

        def put(i, j, value, m=m):
            out[m, i * q : (i + 1) * q, j * q : (j + 1) * q] = value

        for n, (i, j) in enumerate(OFF):
            value = piece(n)
            put(i, j, value)
            put(j, i, value.T)
        for h in range(2):
            value = piece(len(OFF) + h)
            turned = value.T
            put(2 * h, 2 * h, jnp.where(rows <= cols, value, turned))
            own = lines[2 * m + h : 2 * m + h + 1, :]
            for c in range(1, (EXTRA // 4)):
                at = 4 * c + 2 * m + h
                own = jnp.where(rank == c, lines[at : at + 1, :], own)
            own = jnp.broadcast_to(own, (q, q)).astype(BF16)
            lower = jnp.where(rows > cols, value, turned)
            put(2 * h + 1, 2 * h + 1, jnp.where(rows == cols, own, lower))


def unpack_roots(rank, packed, block):
    return pl.pallas_call(
        unpack_kernel,
        in_specs=[pl.BlockSpec(memory_space=pltpu.SMEM), pl.BlockSpec(memory_space=pltpu.VMEM)],
        out_specs=pl.BlockSpec(memory_space=pltpu.VMEM),
        out_shape=jax.ShapeDtypeStruct((2, block, block), BF16),
        compiler_params=params(),
        cost_estimate=cost(0, 8 * block * block),
        name="unpack_roots",
    )(rank, packed)


def update_kernel(roots, grad, out):
    twisted = dot(grad[...], roots[1], 1, 0).astype(BF16)
    out[...] = dot(roots[0], twisted, 1, 0).astype(BF16)


def precondition(roots, grad):
    block = grad.shape[-1]
    return pl.pallas_call(
        update_kernel,
        out_shape=jax.ShapeDtypeStruct(grad.shape, BF16),
        compiler_params=params(),
        cost_estimate=cost(4 * block**3, 8 * block * block),
        name="precondition",
    )(roots, grad)


def gram_kernel(grads, left, right, left_out, right_out):
    block = left.shape[-1]
    grad = grads[...].reshape(block, block)
    gram = dot(grad, grad, 1, 1)
    left_out[...] = (left[...].astype(F32) * DECAY_RATE + gram / block).astype(BF16)
    gram = dot(grad, grad, 0, 0)
    right_out[...] = (right[...].astype(F32) * DECAY_RATE + gram / block).astype(BF16)


def grams(grads, left, right):
    parts, cap, rows, block = grads.shape
    stat = pl.BlockSpec((None, block, block), lambda c: (c, 0, 0))
    return pl.pallas_call(
        gram_kernel,
        grid=(cap,),
        in_specs=[pl.BlockSpec((parts, None, rows, block), lambda c: (0, c, 0, 0)), stat, stat],
        out_specs=[stat, stat],
        out_shape=[jax.ShapeDtypeStruct(left.shape, BF16)] * 2,
        compiler_params=params(),
        cost_estimate=cost(4 * cap * block**3, 10 * cap * block * block),
        name="grams",
    )(grads, left, pltpu.with_memory_space_constraint(right, pltpu.HBM))


def total(*terms):
    return functools.reduce(jnp.add, [t.astype(F32) for t in terms]).astype(BF16)


def fold_kernel(*refs):
    terms, outs = refs[:-SIDE], refs[-SIDE:]
    for t, out in enumerate(outs):
        out[...] = total(*[term[t] for term in terms])


def fold(own, *terms):
    _, half, block = own.shape
    return pl.pallas_call(
        fold_kernel,
        out_shape=[jax.ShapeDtypeStruct((half, block), BF16)] * SIDE,
        compiler_params=params(),
        cost_estimate=cost(0, 8 * half * block),
        name="fold",
    )(pltpu.with_memory_space_constraint(own, pltpu.HBM), *terms)


def finish_kernel(*refs):
    refs[-1][...] = total(*[t[...] for t in refs[-1 - SIDE : -1]])


def finish(terms, at, rest=None):
    half, block = terms[0].shape
    spec = pl.BlockSpec((half, block), lambda i: (0, 0))
    return pl.pallas_call(
        finish_kernel,
        grid=(1,),
        in_specs=([] if rest is None else [pl.BlockSpec(memory_space=pl.ANY)]) + [spec] * SIDE,
        out_specs=pl.BlockSpec((half, block), lambda i: (at, 0)),
        out_shape=jax.ShapeDtypeStruct((2 * half, block), BF16),
        input_output_aliases={} if rest is None else {0: 0},
        compiler_params=params(),
        cost_estimate=cost(0, 10 * half * block),
        name="finish",
    )(*([] if rest is None else [rest]), *terms)


def shards(inputs, output_grads, owner_map, left_stats, right_stats, left_roots, right_roots):
    block = left_stats.shape[-1]
    cap = left_stats.shape[2]
    opt_count = lax.axis_size("opt")
    shard = lax.axis_index("opt")
    home = lax.axis_index("dp")
    chooser = (shard * 4 // opt_count == 3).astype(jnp.int32)
    place = jnp.stack([chooser, home // SIDE, home % SIDE])

    owners = owner_map[0]
    places = jnp.arange(opt_count, dtype=jnp.int32)
    same = (owners[None, :] == owners[:, None]) & (places[None, :] < places[:, None])
    slots = owners * cap + jnp.sum(same.astype(jnp.int32), axis=1)
    slot_ids = jnp.arange(opt_count * cap, dtype=jnp.int32)
    holders = slots[None, :] == slot_ids[:, None]
    homes = jnp.sum(jnp.where(holders, places[None, :] + 1, 0), axis=1) - 1

    a2, b2 = partials(inputs, output_grads, place, (2,), block, weight=WEIGHT)
    place, a2, b2 = lax.optimization_barrier((place, a2, b2))
    a1, b1, a3, b3 = partials(inputs, output_grads, place, (1, 3), block, weight=WEIGHT)

    def send(value, ring):
        return lax.ppermute(value, "dp", ring)

    left_roots, right_roots, _ = lax.optimization_barrier((left_roots, right_roots, a2))
    packed = pack_roots(left_roots[0, 0], right_roots[0, 0], opt_count)
    spread = lax.all_to_all(packed, "opt", 0, 0, tiled=True)

    a_two, b_two = send(a2, x_ring(2)), send(b2, y_ring(2))
    a_terms = [send(a1, x_ring(1)), send(a3, x_ring(3))]
    b_terms = [send(b1, y_ring(1)), send(b3, y_ring(3))]
    a0, b0 = partials(inputs, output_grads, place, (0,), block, (a_two, b_two))

    spread, a0, b0 = lax.optimization_barrier((spread, a0, b0))
    chosen = pick_roots(slots, spread, cap)
    a_terms, b_terms, _ = lax.optimization_barrier((a_terms, b_terms, chosen))
    a_units, b_units = fold(a0, *a_terms), fold(b0, *b_terms)

    b_terms = [b_units[0]] + [send(b_units[t], x_ring(t)) for t in (2, 1, 3)]
    a_terms = [a_units[0]] + [send(a_units[t], y_ring(t)) for t in (2, 1, 3)]

    gathered = lax.all_to_all(chosen, "opt", 0, 0, tiled=True)
    rank = lax.dynamic_slice(slots, (shard,), (1,)) % cap
    roots = unpack_roots(rank, gathered, block)

    grad = finish(a_terms, 0, finish(b_terms, 1))
    grad, roots = lax.optimization_barrier((grad, roots))

    rows = block // opt_count
    spread = lax.all_to_all(grad.reshape(opt_count, rows, block), "opt", 0, 0, tiled=True)
    picked = pick(homes, spread).reshape(opt_count, cap, rows, block)
    owned = lax.all_to_all(picked, "opt", 0, 0, tiled=True)
    update = precondition(roots, grad)
    left_updated, right_updated = grams(owned, left_stats[0, 0], right_stats[0, 0])
    return update[None, None], left_updated[None, None], right_updated[None, None]


def solution(mesh):
    return jax.shard_map(
        shards,
        mesh=mesh,
        in_specs=(
            P(None, "dp", None),
            P("dp", "opt"),
            P("dp", None),
            P("dp", "opt", None, None, None),
            P("dp", "opt", None, None, None),
            P("dp", "opt", None, None, None),
            P("dp", "opt", None, None, None),
        ),
        out_specs=(
            P("opt", "dp", None, None),
            P("dp", "opt", None, None, None),
            P("dp", "opt", None, None, None),
        ),
        check_vma=False,
    )
```

profile of v0, /device:TPU:1, one launch (start us, length us, event | category | flops | bytes accessed | tf_op | source)
XLA Modules:
  0.0 145.4 jit_solution(1222837129897502751)
XLA Ops:
  0.7 5.0 %partials.3 = (bf16[4,256,512]{2,1,0:T(8,128)(2,1)}, bf16[4,256,512]{2,1,0:T(8,128)(2,1)}) custom-call(s32[3]{0:T(128)S(1)} %pad_add_fusion.place, bf16[2,512,4096]{2,1,0:T(8,128)(2,1)} %source.5, bf16[512,1024]{1,0:T(8,128)(2,1)} %target.5), custom_call_target="tpu_custom_call" | custom-call | flops 107374182400 | bytes 7340032 | tf_op jit(solution)/shard_map/partials/pallas_call | solution.py:122
  5.8 3.6 %collective-permute-start = (bf16[4,256,512]{2,1,0:T(8,128)(2,1)}, bf16[4,256,512]{2,1,0:T(8,128)(2,1)}, u32[]{:S(2)}, u32[]{:S(2)}) collective-permute-start(bf16[4,256,512]{2,1,0:T(8,128)(2,1)} %get-tuple-element.37), channel_id=1, source_target_pairs={{0,32},{16,48},{32,0},{48,16},{64,96},{80,112},{96,64},{112,80},{1... | collective-permute-start | bytes 3145736 | tf_op jit(solution)/shard_map/ppermute | solution.py:388
  9.4 2.9 %collective-permute-start.1 = (bf16[4,256,512]{2,1,0:T(8,128)(2,1)}, bf16[4,256,512]{2,1,0:T(8,128)(2,1)}, u32[]{:S(2)}, u32[]{:S(2)}) collective-permute-start(bf16[4,256,512]{2,1,0:T(8,128)(2,1)} %get-tuple-element.41), channel_id=1, source_target_pairs={{0,128},{16,144},{32,160},{48,176},{64,192},{80,208},{96,224},{112... | collective-permute-start | bytes 3145736 | tf_op jit(solution)/shard_map/ppermute | solution.py:388
  12.3 1.2 pack_roots.1
  13.6 9.7 %all-to-all-start = ((bf16[16,272,128]{2,1,0:T(8,128)(2,1)}), bf16[16,272,128]{2,1,0:T(8,128)(2,1)}, u32[]{:S(2)}, u32[]{:S(2)}) async-start(bf16[16,272,128]{2,1,0:T(8,128)(2,1)} %pack_roots.1), calls=%async_computation | async-start | bytes 2228224 | tf_op jit(solution)/shard_map/all_to_all | solution.py:392
  23.3 7.2 %partials.5 = (bf16[4,256,512]{2,1,0:T(8,128)(2,1)}, bf16[4,256,512]{2,1,0:T(8,128)(2,1)}, bf16[4,256,512]{2,1,0:T(8,128)(2,1)}, bf16[4,256,512]{2,1,0:T(8,128)(2,1)}) custom-call(s32[3]{0:T(128)S(1)} %pad_add_fusion.place, bf16[2,512,4096]{2,1,0:T(8,128)(2,1)} %source.5, bf16[512,1024]{1,0:T(8,128)(2,1)} %target.5), custom_call_target="tpu_custom_call" | custom-call | flops 214748364800 | bytes 9437184 | tf_op jit(solution)/shard_map/partials/pallas_call | solution.py:122
  30.5 0.4 collective-permute-start.2
  30.9 2.4 %collective-permute-start.3 = (bf16[4,256,512]{2,1,0:T(8,128)(2,1)}, bf16[4,256,512]{2,1,0:T(8,128)(2,1)S(1)}, u32[]{:S(2)}, u32[]{:S(2)}) collective-permute-start(bf16[4,256,512]{2,1,0:T(8,128)(2,1)} %get-tuple-element.46), channel_id=1, source_target_pairs={{0,48},{16,0},{32,16},{48,32},{64,112},{80,64},{96,80},{112,96},{1... | collective-permute-start | bytes 3145736 | tf_op jit(solution)/shard_map/ppermute | solution.py:388
  33.2 0.4 collective-permute-start.4
  33.7 2.3 %collective-permute-start.5 = (bf16[4,256,512]{2,1,0:T(8,128)(2,1)}, bf16[4,256,512]{2,1,0:T(8,128)(2,1)}, u32[]{:S(2)}, u32[]{:S(2)}) collective-permute-start(bf16[4,256,512]{2,1,0:T(8,128)(2,1)} %get-tuple-element.48), channel_id=1, source_target_pairs={{0,192},{16,208},{32,224},{48,240},{64,0},{80,16},{96,32},{112,48}... | collective-permute-start | bytes 3145736 | tf_op jit(solution)/shard_map/ppermute | solution.py:388
  36.1 5.9 %partials.4 = (bf16[4,256,512]{2,1,0:T(8,128)(2,1)}, bf16[4,256,512]{2,1,0:T(8,128)(2,1)}) custom-call(s32[3]{0:T(128)S(1)} %pad_add_fusion.place, bf16[2,512,4096]{2,1,0:T(8,128)(2,1)} %source.5, bf16[512,1024]{1,0:T(8,128)(2,1)} %target.5, bf16[4,256,512]{2,1,0:T(8,128)(2,1)} %collective-permute-done.refs_0_, ...), custom_call_target="tpu_custom_call" | custom-call | flops 1073741824 | bytes 7340032 | tf_op jit(solution)/shard_map/partials/pallas_call | solution.py:122
  42.0 10.7 %all-to-all-done.src = bf16[16,272,128]{2,1,0:T(8,128)(2,1)} async-done(((bf16[16,272,128]{2,1,0:T(8,128)(2,1)}), bf16[16,272,128]{2,1,0:T(8,128)(2,1)}, u32[]{:S(2)}, u32[]{:S(2)}) %all-to-all-start) | async-done | bytes 1114144 | tf_op jit(solution)/shard_map/all_to_all | solution.py:392
  52.7 2.2 %pick_roots.1 = bf16[16,144,128]{2,1,0:T(8,128)(2,1)} custom-call(s32[16]{0:T(128)S(1)} %multiply_add_fusion.slots, bf16[16,272,128]{2,1,0:T(8,128)(2,1)} %all-to-all-done.src), custom_call_target="tpu_custom_call" | custom-call | bytes 2228224 | tf_op jit(solution)/shard_map/pick_roots/pallas_call | solution.py:204
  54.8 3.6 %all-to-all-start.1 = ((bf16[16,144,128]{2,1,0:T(8,128)(2,1)}), bf16[16,144,128]{2,1,0:T(8,128)(2,1)S(1)}, u32[]{:S(2)}, u32[]{:S(2)}) async-start(bf16[16,144,128]{2,1,0:T(8,128)(2,1)} %pick_roots.1), calls=%async_computation.1 | async-start | bytes 1179648 | tf_op jit(solution)/shard_map/all_to_all | solution.py:407
  58.7 2.8 %fold.2 = (bf16[256,512]{1,0:T(8,128)(2,1)S(1)}, bf16[256,512]{1,0:T(8,128)(2,1)}, bf16[256,512]{1,0:T(8,128)(2,1)S(1)}, bf16[256,512]{1,0:T(8,128)(2,1)}) custom-call(bf16[4,256,512]{2,1,0:T(8,128)(2,1)} %get-tuple-element.44.refs_0_, bf16[4,256,512]{2,1,0:T(8,128)(2,1)} %collective-permute-done.4.refs_1_, bf16[4,256,512]{2,1,0:T(8,128)(2,1)} %collective-permute-done.5.refs_2_), custom_call_target="tpu_custom_call" | custom-call | bytes 1048576 | tf_op jit(solution)/shard_map/fold/pallas_call | solution.py:337
  61.7 2.2 %fold.3 = (bf16[256,512]{1,0:T(8,128)(2,1)S(1)}, bf16[256,512]{1,0:T(8,128)(2,1)}, bf16[256,512]{1,0:T(8,128)(2,1)}, bf16[256,512]{1,0:T(8,128)(2,1)}) custom-call(bf16[4,256,512]{2,1,0:T(8,128)(2,1)} %get-tuple-element.56.refs_0_, bf16[4,256,512]{2,1,0:T(8,128)(2,1)S(1)} %collective-permute-done.2.refs_1_, ...), custom_call_target="tpu_custom_call" | custom-call | bytes 1048576 | tf_op jit(solution)/shard_map/fold/pallas_call | solution.py:337
  63.9 1.3 collective-permute-start.10
  65.2 0.5 collective-permute-start.7
  65.7 2.2 %collective-permute-start.8 = (bf16[256,512]{1,0:T(8,128)(2,1)}, bf16[256,512]{1,0:T(8,128)(2,1)S(1)}, u32[]{:S(2)}, u32[]{:S(2)}) collective-permute-start(bf16[256,512]{1,0:T(8,128)(2,1)} %get-tuple-element.55), channel_id=1, source_target_pairs={{0,48},{16,0},{32,16},{48,32},{64,112},{80,64},{96,80},{112,96},{1... | collective-permute-start | bytes 786440 | tf_op jit(solution)/shard_map/ppermute | solution.py:388
  67.9 1.4 collective-permute-start.11
  69.3 4.1 %collective-permute-start.9 = (bf16[256,512]{1,0:T(8,128)(2,1)}, bf16[256,512]{1,0:T(8,128)(2,1)S(1)}, u32[]{:S(2)}, u32[]{:S(2)}) collective-permute-start(bf16[256,512]{1,0:T(8,128)(2,1)} %get-tuple-element.60), channel_id=1, source_target_pairs={{0,128},{16,144},{32,160},{48,176},{64,192},{80,208},{96,224},{112... | collective-permute-start | bytes 786440 | tf_op jit(solution)/shard_map/ppermute | solution.py:388
  73.4 0.6 dynamic_slice.3
  76.0 0.8 finish.2.refs_0_
  76.8 2.6 %collective-permute-done.9.refs_2_ = bf16[256,512]{1,0:T(8,128)(2,1)S(1)} collective-permute-done((bf16[256,512]{1,0:T(8,128)(2,1)}, bf16[256,512]{1,0:T(8,128)(2,1)S(1)}, u32[]{:S(2)}, u32[]{:S(2)}) %collective-permute-start.9) | collective-permute-done | bytes 262176 | tf_op jit(solution)/shard_map/ppermute | solution.py:388
  79.4 0.8 finish.3.grad
  80.4 11.5 %all-to-all-start.2 = ((bf16[16,32,512]{2,1,0:T(8,128)(2,1)}), bf16[16,32,512]{2,1,0:T(8,128)(2,1)S(1)}, u32[]{:S(2)}, u32[]{:S(2)}) async-start(bf16[16,32,512]{2,1,0:T(8,128)(2,1)} %bitcast.9), calls=%async_computation.2 | async-start | bytes 1048576 | tf_op jit(solution)/shard_map/all_to_all | solution.py:415
  92.0 17.2 %all-to-all-done.2.src = bf16[16,32,512]{2,1,0:T(8,128)(2,1)S(1)} async-done(((bf16[16,32,512]{2,1,0:T(8,128)(2,1)}), bf16[16,32,512]{2,1,0:T(8,128)(2,1)S(1)}, u32[]{:S(2)}, u32[]{:S(2)}) %all-to-all-start.2) | async-done | bytes 524320 | tf_op jit(solution)/shard_map/all_to_all | solution.py:415
  109.2 1.9 %pick.1 = bf16[32,32,512]{2,1,0:T(8,128)(2,1)} custom-call(s32[32]{0:T(128)S(1)} %broadcast_add_fusion.index, bf16[16,32,512]{2,1,0:T(8,128)(2,1)S(1)} %all-to-all-done.2.src), custom_call_target="tpu_custom_call" | custom-call | bytes 1048576 | tf_op jit(solution)/shard_map/pick/pallas_call | solution.py:230
  111.2 3.6 %all-to-all-start.3 = ((bf16[16,2,32,512]{3,2,1,0:T(8,128)(2,1)}), bf16[16,2,32,512]{3,2,1,0:T(8,128)(2,1)S(1)}, u32[]{:S(2)}, u32[]{:S(2)}) async-start(bf16[16,2,32,512]{3,2,1,0:T(8,128)(2,1)} %bitcast.10), calls=%async_computation.3 | async-start | bytes 2097152 | tf_op jit(solution)/shard_map/all_to_all | solution.py:417
  114.7 2.7 %precondition.1 = bf16[512,512]{1,0:T(8,128)(2,1)} custom-call(bf16[2,512,512]{2,1,0:T(8,128)(2,1)S(1)} %unpack_roots.1.roots, bf16[512,512]{1,0:T(8,128)(2,1)} %finish.3.grad), custom_call_target="tpu_custom_call" | custom-call | flops 536870912 | bytes 2097152 | tf_op jit(solution)/shard_map/precondition/pallas_call | solution.py:292
  117.5 24.6 %all-to-all-done.3.grads = bf16[16,2,32,512]{3,2,1,0:T(8,128)(2,1)S(1)} async-done(((bf16[16,2,32,512]{3,2,1,0:T(8,128)(2,1)}), bf16[16,2,32,512]{3,2,1,0:T(8,128)(2,1)S(1)}, u32[]{:S(2)}, u32[]{:S(2)}) %all-to-all-start.3) | async-done | bytes 1048608 | tf_op jit(solution)/shard_map/all_to_all | solution.py:417
  142.0 3.4 %grams.1 = (bf16[2,512,512]{2,1,0:T(8,128)(2,1)}, bf16[2,512,512]{2,1,0:T(8,128)(2,1)}) custom-call(bf16[16,2,32,512]{3,2,1,0:T(8,128)(2,1)S(1)} %all-to-all-done.3.grads, bf16[2,512,512]{2,1,0:T(8,128)(2,1)S(1)} %bitcast.22, bf16[2,512,512]{2,1,0:T(8,128)(2,1)} %bitcast.24), custom_call_target="tpu_custom_call" | custom-call | flops 1073741824 | bytes 5242880 | tf_op jit(solution)/shard_map/grams/pallas_call | solution.py:313
  (29 shorter events, 1.1 us)
Async XLA Ops:
  0.7 11.6 %copy-start = (bf16[1,1,2,512,512]{4,3,2,1,0:T(8,128)(2,1)S(1)}, bf16[1,1,2,512,512]{4,3,2,1,0:T(8,128)(2,1)}, u32[]{:S(2)}) copy-start(bf16[1,1,2,512,512]{4,3,2,1,0:T(8,128)(2,1)} %param.12) | copy-start | bytes 3145732
  0.7 11.6 %copy-start.1 = (bf16[1,1,2,512,512]{4,3,2,1,0:T(8,128)(2,1)S(1)}, bf16[1,1,2,512,512]{4,3,2,1,0:T(8,128)(2,1)}, u32[]{:S(2)}) copy-start(bf16[1,1,2,512,512]{4,3,2,1,0:T(8,128)(2,1)} %param.13) | copy-start | bytes 3145732
  5.8 27.9 %collective-permute-start = (bf16[4,256,512]{2,1,0:T(8,128)(2,1)}, bf16[4,256,512]{2,1,0:T(8,128)(2,1)}, u32[]{:S(2)}, u32[]{:S(2)}) collective-permute-start(bf16[4,256,512]{2,1,0:T(8,128)(2,1)} %get-tuple-element.37), channel_id=1, source_target_pairs={{0,32},{16,48},{32,0},{48,16},{64,96},{80,112},{96,64},{112,80},{1... | collective-permute-start | bytes 3145736 | tf_op jit(solution)/shard_map/ppermute | solution.py:388
  9.4 26.7 %collective-permute-start.1 = (bf16[4,256,512]{2,1,0:T(8,128)(2,1)}, bf16[4,256,512]{2,1,0:T(8,128)(2,1)}, u32[]{:S(2)}, u32[]{:S(2)}) collective-permute-start(bf16[4,256,512]{2,1,0:T(8,128)(2,1)} %get-tuple-element.41), channel_id=1, source_target_pairs={{0,128},{16,144},{32,160},{48,176},{64,192},{80,208},{96,224},{112... | collective-permute-start | bytes 3145736 | tf_op jit(solution)/shard_map/ppermute | solution.py:388
  13.6 39.1 %all-to-all-start = ((bf16[16,272,128]{2,1,0:T(8,128)(2,1)}), bf16[16,272,128]{2,1,0:T(8,128)(2,1)}, u32[]{:S(2)}, u32[]{:S(2)}) async-start(bf16[16,272,128]{2,1,0:T(8,128)(2,1)} %pack_roots.1), calls=%async_computation | async-start | bytes 2228224 | tf_op jit(solution)/shard_map/all_to_all | solution.py:392
  23.3 12.6 %copy-start.3 = (s32[1,16]{1,0:T(1,128)S(1)}, s32[1,16]{1,0:T(1,128)}, u32[]{:S(2)}) copy-start(s32[1,16]{1,0:T(1,128)} %param.9) | copy-start | bytes 196
  30.5 27.9 %collective-permute-start.2 = (bf16[4,256,512]{2,1,0:T(8,128)(2,1)}, bf16[4,256,512]{2,1,0:T(8,128)(2,1)S(1)}, u32[]{:S(2)}, u32[]{:S(2)}) collective-permute-start(bf16[4,256,512]{2,1,0:T(8,128)(2,1)} %get-tuple-element.45), channel_id=1, source_target_pairs={{0,16},{16,32},{32,48},{48,0},{64,80},{80,96},{96,112},{112,64},{1... | collective-permute-start | bytes 3145736 | tf_op jit(solution)/shard_map/ppermute | solution.py:388
  30.9 27.6 %collective-permute-start.3 = (bf16[4,256,512]{2,1,0:T(8,128)(2,1)}, bf16[4,256,512]{2,1,0:T(8,128)(2,1)S(1)}, u32[]{:S(2)}, u32[]{:S(2)}) collective-permute-start(bf16[4,256,512]{2,1,0:T(8,128)(2,1)} %get-tuple-element.46), channel_id=1, source_target_pairs={{0,48},{16,0},{32,16},{48,32},{64,112},{80,64},{96,80},{112,96},{1... | collective-permute-start | bytes 3145736 | tf_op jit(solution)/shard_map/ppermute | solution.py:388
  33.2 25.5 %collective-permute-start.4 = (bf16[4,256,512]{2,1,0:T(8,128)(2,1)}, bf16[4,256,512]{2,1,0:T(8,128)(2,1)}, u32[]{:S(2)}, u32[]{:S(2)}) collective-permute-start(bf16[4,256,512]{2,1,0:T(8,128)(2,1)} %get-tuple-element.47), channel_id=1, source_target_pairs={{0,64},{16,80},{32,96},{48,112},{64,128},{80,144},{96,160},{112,17... | collective-permute-start | bytes 3145736 | tf_op jit(solution)/shard_map/ppermute | solution.py:388
  33.7 25.1 %collective-permute-start.5 = (bf16[4,256,512]{2,1,0:T(8,128)(2,1)}, bf16[4,256,512]{2,1,0:T(8,128)(2,1)}, u32[]{:S(2)}, u32[]{:S(2)}) collective-permute-start(bf16[4,256,512]{2,1,0:T(8,128)(2,1)} %get-tuple-element.48), channel_id=1, source_target_pairs={{0,192},{16,208},{32,224},{48,240},{64,0},{80,16},{96,32},{112,48}... | collective-permute-start | bytes 3145736 | tf_op jit(solution)/shard_map/ppermute | solution.py:388
  54.8 25.4 %all-to-all-start.1 = ((bf16[16,144,128]{2,1,0:T(8,128)(2,1)}), bf16[16,144,128]{2,1,0:T(8,128)(2,1)S(1)}, u32[]{:S(2)}, u32[]{:S(2)}) async-start(bf16[16,144,128]{2,1,0:T(8,128)(2,1)} %pick_roots.1), calls=%async_computation.1 | async-start | bytes 1179648 | tf_op jit(solution)/shard_map/all_to_all | solution.py:407
  61.5 7.8 %collective-permute-start.6 = (bf16[256,512]{1,0:T(8,128)(2,1)S(1)}, bf16[256,512]{1,0:T(8,128)(2,1)S(1)}, u32[]{:S(2)}, u32[]{:S(2)}) collective-permute-start(bf16[256,512]{1,0:T(8,128)(2,1)S(1)} %get-tuple-element.53), channel_id=1, source_target_pairs={{0,32},{16,48},{32,0},{48,16},{64,96},{80,112},{96,64},{112,80},{1... | collective-permute-start | bytes 786440 | tf_op jit(solution)/shard_map/ppermute | solution.py:388
  63.9 12.9 %collective-permute-start.10 = (bf16[256,512]{1,0:T(8,128)(2,1)}, bf16[256,512]{1,0:T(8,128)(2,1)S(1)}, u32[]{:S(2)}, u32[]{:S(2)}) collective-permute-start(bf16[256,512]{1,0:T(8,128)(2,1)} %get-tuple-element.61), channel_id=1, source_target_pairs={{0,64},{16,80},{32,96},{48,112},{64,128},{80,144},{96,160},{112,17... | collective-permute-start | bytes 786440 | tf_op jit(solution)/shard_map/ppermute | solution.py:388
  65.2 10.7 %collective-permute-start.7 = (bf16[256,512]{1,0:T(8,128)(2,1)}, bf16[256,512]{1,0:T(8,128)(2,1)S(1)}, u32[]{:S(2)}, u32[]{:S(2)}) collective-permute-start(bf16[256,512]{1,0:T(8,128)(2,1)} %get-tuple-element.54), channel_id=1, source_target_pairs={{0,16},{16,32},{32,48},{48,0},{64,80},{80,96},{96,112},{112,64},{1... | collective-permute-start | bytes 786440 | tf_op jit(solution)/shard_map/ppermute | solution.py:388
  65.7 10.3 %collective-permute-start.8 = (bf16[256,512]{1,0:T(8,128)(2,1)}, bf16[256,512]{1,0:T(8,128)(2,1)S(1)}, u32[]{:S(2)}, u32[]{:S(2)}) collective-permute-start(bf16[256,512]{1,0:T(8,128)(2,1)} %get-tuple-element.55), channel_id=1, source_target_pairs={{0,48},{16,0},{32,16},{48,32},{64,112},{80,64},{96,80},{112,96},{1... | collective-permute-start | bytes 786440 | tf_op jit(solution)/shard_map/ppermute | solution.py:388
  67.9 8.9 %collective-permute-start.11 = (bf16[256,512]{1,0:T(8,128)(2,1)}, bf16[256,512]{1,0:T(8,128)(2,1)S(1)}, u32[]{:S(2)}, u32[]{:S(2)}) collective-permute-start(bf16[256,512]{1,0:T(8,128)(2,1)} %get-tuple-element.62), channel_id=1, source_target_pairs={{0,192},{16,208},{32,224},{48,240},{64,0},{80,16},{96,32},{112,48}... | collective-permute-start | bytes 786440 | tf_op jit(solution)/shard_map/ppermute | solution.py:388
  69.3 10.1 %collective-permute-start.9 = (bf16[256,512]{1,0:T(8,128)(2,1)}, bf16[256,512]{1,0:T(8,128)(2,1)S(1)}, u32[]{:S(2)}, u32[]{:S(2)}) collective-permute-start(bf16[256,512]{1,0:T(8,128)(2,1)} %get-tuple-element.60), channel_id=1, source_target_pairs={{0,128},{16,144},{32,160},{48,176},{64,192},{80,208},{96,224},{112... | collective-permute-start | bytes 786440 | tf_op jit(solution)/shard_map/ppermute | solution.py:388
  80.4 28.8 %all-to-all-start.2 = ((bf16[16,32,512]{2,1,0:T(8,128)(2,1)}), bf16[16,32,512]{2,1,0:T(8,128)(2,1)S(1)}, u32[]{:S(2)}, u32[]{:S(2)}) async-start(bf16[16,32,512]{2,1,0:T(8,128)(2,1)} %bitcast.9), calls=%async_computation.2 | async-start | bytes 1048576 | tf_op jit(solution)/shard_map/all_to_all | solution.py:415
  111.2 30.8 %all-to-all-start.3 = ((bf16[16,2,32,512]{3,2,1,0:T(8,128)(2,1)}), bf16[16,2,32,512]{3,2,1,0:T(8,128)(2,1)S(1)}, u32[]{:S(2)}, u32[]{:S(2)}) async-start(bf16[16,2,32,512]{3,2,1,0:T(8,128)(2,1)} %bitcast.10), calls=%async_computation.3 | async-start | bytes 2097152 | tf_op jit(solution)/shard_map/all_to_all | solution.py:417
  114.7 27.3 %copy-start.2 = (bf16[1,1,2,512,512]{4,3,2,1,0:T(8,128)(2,1)S(1)}, bf16[1,1,2,512,512]{4,3,2,1,0:T(8,128)(2,1)}, u32[]{:S(2)}) copy-start(bf16[1,1,2,512,512]{4,3,2,1,0:T(8,128)(2,1)} %param.10) | copy-start | bytes 3145732
where the time goes:
time: 146 us; the launch traced here: 145 us
  waiting for transfers between devices  55.3 us (38%)
  starting transfers between devices  50 us (34%)
  Pallas kernels  36.4 us (25%)
  between operations  2.74 us (2%)
    all_to_all x1, waiting for transfers between devices, shards(): owned = lax.all_to_all(picked, 'opt', 0, 0, tiled=True)  24.6 us
    ppermute x12, starting transfers between devices, send(): return lax.ppermute(value, 'dp', ring)  21.6 us
    pallas_call x3, Pallas kernels, partials(): pl.pallas_call(functools.partial(partial_kernel, steps), in_specs=[pl.Blo...  18.1 us
    all_to_all x1, waiting for transfers between devices, shards(): lax.all_to_all(grad.reshape(opt_count, rows, block), 'opt', 0, 0, tiled=T...  17.2 us
    all_to_all x1, starting transfers between devices, shards(): lax.all_to_all(grad.reshape(opt_count, rows, block), 'opt', 0, 0, tiled=T...  11.5 us
    all_to_all x1, waiting for transfers between devices, shards(): spread = lax.all_to_all(packed, 'opt', 0, 0, tiled=True)  10.7 us
    all_to_all x1, starting transfers between devices, shards(): spread = lax.all_to_all(packed, 'opt', 0, 0, tiled=True)  9.72 us
    pallas_call x2, Pallas kernels, fold(): pl.pallas_call(fold_kernel, out_shape=[jax.ShapeDtypeStruct((half, block)...  5.01 us
  transfers between devices with their start and end apart: 16, of which 5 were waited for; matrix products, arithmetic and copies ran while one was open for 1% of the time, Pallas kernels for 18%

commit v1 on v0

--- a/solution.py
+++ b/solution.py
@@ -37,7 +37,13 @@
     return lax.dot_general(a, b, (((over_a,), (over_b,)), ((), ())), preferred_element_type=F32)
 
 
-def partial_kernel(steps, place, source, target, *refs):
+def position():
+    home = lax.axis_index("dp")
+    fourth = lax.div(lax.axis_index("opt") * 4, lax.axis_size("opt"))
+    return (fourth == 3).astype(jnp.int32), lax.div(home, SIDE), lax.rem(home, SIDE)
+
+
+def partial_kernel(steps, inside, place, source, target, *refs):
     count = 2 * len(steps)
     extra = (len(refs) - 5 - 2 * count) // 2
     terms, results = refs[:extra], refs[extra : extra + count]
@@ -45,7 +51,7 @@
     rows, cols, sems, out_sems, term_sems = refs[-5:]
     block = cols.shape[1] // 2
     half = block // 2
-    chooser, y, x = place[0], place[1], place[2]
+    chooser, y, x = position() if inside else (place[0], place[1], place[2])
 
     def units_of(r, along_x):
         for t in range(SIDE):
@@ -120,7 +126,7 @@
     shape = (SIDE, half, block)
     hbm = pl.BlockSpec(memory_space=pltpu.HBM)
     return pl.pallas_call(
-        functools.partial(partial_kernel, steps),
+        functools.partial(partial_kernel, steps, place is None),
         in_specs=[pl.BlockSpec(memory_space=pltpu.SMEM)] + [hbm] * (2 + len(terms)),
         out_specs=[hbm] * count,
         out_shape=[pltpu.HBM(shape, BF16)] * count,
@@ -138,7 +144,7 @@
             2 * (tok * feats + output_grads.size + units * half * block),
         ),
         name="partials",
-    )(place, *[pltpu.with_memory_space_constraint(a, pltpu.HBM) for a in (inputs, output_grads, *terms)])
+    )(jnp.zeros((3,), jnp.int32) if place is None else place, *[pltpu.with_memory_space_constraint(a, pltpu.HBM) for a in (inputs, output_grads, *terms)])
 
 
 def grid_masks(n):
@@ -368,9 +374,7 @@
     cap = left_stats.shape[2]
     opt_count = lax.axis_size("opt")
     shard = lax.axis_index("opt")
-    home = lax.axis_index("dp")
-    chooser = (shard * 4 // opt_count == 3).astype(jnp.int32)
-    place = jnp.stack([chooser, home // SIDE, home % SIDE])
+    place = jnp.stack(position())
 
     owners = owner_map[0]
     places = jnp.arange(opt_count, dtype=jnp.int32)
@@ -380,7 +384,7 @@
     holders = slots[None, :] == slot_ids[:, None]
     homes = jnp.sum(jnp.where(holders, places[None, :] + 1, 0), axis=1) - 1
 
-    a2, b2 = partials(inputs, output_grads, place, (2,), block, weight=WEIGHT)
+    a2, b2 = partials(inputs, output_grads, None, (2,), block, weight=WEIGHT)
     place, a2, b2 = lax.optimization_barrier((place, a2, b2))
     a1, b1, a3, b3 = partials(inputs, output_grads, place, (1, 3), block, weight=WEIGHT)
 

time: 146 us -> 146 us (level)
  no operation moved by 1% of the time
where the time goes in v1:
time: 146 us; the launch traced here: 145 us
  waiting for transfers between devices  55.3 us (38%)
  starting transfers between devices  50 us (34%)
  Pallas kernels  36.4 us (25%)
  between operations  2.71 us (2%)
    all_to_all x1, waiting for transfers between devices, shards(): owned = lax.all_to_all(picked, 'opt', 0, 0, tiled=True)  24.6 us
    ppermute x12, starting transfers between devices, send(): return lax.ppermute(value, 'dp', ring)  21.6 us
    pallas_call x3, Pallas kernels, partials(): pl.pallas_call(functools.partial(partial_kernel, steps, place is None), i...  18 us
    all_to_all x1, waiting for transfers between devices, shards(): lax.all_to_all(grad.reshape(opt_count, rows, block), 'opt', 0, 0, tiled=T...  17.2 us
    all_to_all x1, starting transfers between devices, shards(): lax.all_to_all(grad.reshape(opt_count, rows, block), 'opt', 0, 0, tiled=T...  11.5 us
    all_to_all x1, waiting for transfers between devices, shards(): spread = lax.all_to_all(packed, 'opt', 0, 0, tiled=True)  10.7 us
    all_to_all x1, starting transfers between devices, shards(): spread = lax.all_to_all(packed, 'opt', 0, 0, tiled=True)  9.71 us
    pallas_call x2, Pallas kernels, fold(): pl.pallas_call(fold_kernel, out_shape=[jax.ShapeDtypeStruct((half, block)...  5.01 us
  transfers between devices with their start and end apart: 16, of which 5 were waited for; matrix products, arithmetic and copies ran while one was open for 1% of the time, Pallas kernels for 18%

profile of v1, /device:TPU:1, one launch (start us, length us, event | category | flops | bytes accessed | tf_op | source)
XLA Modules:
  0.0 145.4 jit_solution(17375128147380235554)
XLA Ops:
  0.7 5.0 %partials.3 = (bf16[4,256,512]{2,1,0:T(8,128)(2,1)}, bf16[4,256,512]{2,1,0:T(8,128)(2,1)}) custom-call(s32[3]{0:T(128)S(1)} %broadcast_3_place.2.place, bf16[2,512,4096]{2,1,0:T(8,128)(2,1)} %source.5, bf16[512,1024]{1,0:T(8,128)(2,1)} %target.5), custom_call_target="tpu_custom_call" | custom-call | flops 107374182400 | bytes 7340032 | tf_op jit(solution)/shard_map/partials/pallas_call | solution.py:128
  5.7 3.6 %collective-permute-start = (bf16[4,256,512]{2,1,0:T(8,128)(2,1)}, bf16[4,256,512]{2,1,0:T(8,128)(2,1)}, u32[]{:S(2)}, u32[]{:S(2)}) collective-permute-start(bf16[4,256,512]{2,1,0:T(8,128)(2,1)} %get-tuple-element.37), channel_id=1, source_target_pairs={{0,32},{16,48},{32,0},{48,16},{64,96},{80,112},{96,64},{112,80},{1... | collective-permute-start | bytes 3145736 | tf_op jit(solution)/shard_map/ppermute | solution.py:392
  9.4 2.9 %collective-permute-start.1 = (bf16[4,256,512]{2,1,0:T(8,128)(2,1)}, bf16[4,256,512]{2,1,0:T(8,128)(2,1)}, u32[]{:S(2)}, u32[]{:S(2)}) collective-permute-start(bf16[4,256,512]{2,1,0:T(8,128)(2,1)} %get-tuple-element.41), channel_id=1, source_target_pairs={{0,128},{16,144},{32,160},{48,176},{64,192},{80,208},{96,224},{112... | collective-permute-start | bytes 3145736 | tf_op jit(solution)/shard_map/ppermute | solution.py:392
  12.3 1.2 pack_roots.1
  13.6 9.7 %all-to-all-start = ((bf16[16,272,128]{2,1,0:T(8,128)(2,1)}), bf16[16,272,128]{2,1,0:T(8,128)(2,1)}, u32[]{:S(2)}, u32[]{:S(2)}) async-start(bf16[16,272,128]{2,1,0:T(8,128)(2,1)} %pack_roots.1), calls=%async_computation | async-start | bytes 2228224 | tf_op jit(solution)/shard_map/all_to_all | solution.py:396
  23.3 7.2 %partials.5 = (bf16[4,256,512]{2,1,0:T(8,128)(2,1)}, bf16[4,256,512]{2,1,0:T(8,128)(2,1)}, bf16[4,256,512]{2,1,0:T(8,128)(2,1)}, bf16[4,256,512]{2,1,0:T(8,128)(2,1)}) custom-call(s32[3]{0:T(128)S(1)} %pad_add_fusion.place, bf16[2,512,4096]{2,1,0:T(8,128)(2,1)} %source.5, bf16[512,1024]{1,0:T(8,128)(2,1)} %target.5), custom_call_target="tpu_custom_call" | custom-call | flops 214748364800 | bytes 9437184 | tf_op jit(solution)/shard_map/partials/pallas_call | solution.py:128
  30.5 0.4 collective-permute-start.2
  30.9 2.4 %collective-permute-start.3 = (bf16[4,256,512]{2,1,0:T(8,128)(2,1)}, bf16[4,256,512]{2,1,0:T(8,128)(2,1)S(1)}, u32[]{:S(2)}, u32[]{:S(2)}) collective-permute-start(bf16[4,256,512]{2,1,0:T(8,128)(2,1)} %get-tuple-element.46), channel_id=1, source_target_pairs={{0,48},{16,0},{32,16},{48,32},{64,112},{80,64},{96,80},{112,96},{1... | collective-permute-start | bytes 3145736 | tf_op jit(solution)/shard_map/ppermute | solution.py:392
  33.2 0.4 collective-permute-start.4
  33.6 2.3 %collective-permute-start.5 = (bf16[4,256,512]{2,1,0:T(8,128)(2,1)}, bf16[4,256,512]{2,1,0:T(8,128)(2,1)}, u32[]{:S(2)}, u32[]{:S(2)}) collective-permute-start(bf16[4,256,512]{2,1,0:T(8,128)(2,1)} %get-tuple-element.48), channel_id=1, source_target_pairs={{0,192},{16,208},{32,224},{48,240},{64,0},{80,16},{96,32},{112,48}... | collective-permute-start | bytes 3145736 | tf_op jit(solution)/shard_map/ppermute | solution.py:392
  36.1 5.8 %partials.4 = (bf16[4,256,512]{2,1,0:T(8,128)(2,1)}, bf16[4,256,512]{2,1,0:T(8,128)(2,1)}) custom-call(s32[3]{0:T(128)S(1)} %pad_add_fusion.place, bf16[2,512,4096]{2,1,0:T(8,128)(2,1)} %source.5, bf16[512,1024]{1,0:T(8,128)(2,1)} %target.5, bf16[4,256,512]{2,1,0:T(8,128)(2,1)} %collective-permute-done.refs_0_, ...), custom_call_target="tpu_custom_call" | custom-call | flops 1073741824 | bytes 7340032 | tf_op jit(solution)/shard_map/partials/pallas_call | solution.py:128
  42.0 10.7 %all-to-all-done.src = bf16[16,272,128]{2,1,0:T(8,128)(2,1)} async-done(((bf16[16,272,128]{2,1,0:T(8,128)(2,1)}), bf16[16,272,128]{2,1,0:T(8,128)(2,1)}, u32[]{:S(2)}, u32[]{:S(2)}) %all-to-all-start) | async-done | bytes 1114144 | tf_op jit(solution)/shard_map/all_to_all | solution.py:396
  52.6 2.2 %pick_roots.1 = bf16[16,144,128]{2,1,0:T(8,128)(2,1)} custom-call(s32[16]{0:T(128)S(1)} %multiply_add_fusion.slots, bf16[16,272,128]{2,1,0:T(8,128)(2,1)} %all-to-all-done.src), custom_call_target="tpu_custom_call" | custom-call | bytes 2228224 | tf_op jit(solution)/shard_map/pick_roots/pallas_call | solution.py:210
  54.8 3.6 %all-to-all-start.1 = ((bf16[16,144,128]{2,1,0:T(8,128)(2,1)}), bf16[16,144,128]{2,1,0:T(8,128)(2,1)S(1)}, u32[]{:S(2)}, u32[]{:S(2)}) async-start(bf16[16,144,128]{2,1,0:T(8,128)(2,1)} %pick_roots.1), calls=%async_computation.1 | async-start | bytes 1179648 | tf_op jit(solution)/shard_map/all_to_all | solution.py:411
  58.7 2.8 %fold.2 = (bf16[256,512]{1,0:T(8,128)(2,1)S(1)}, bf16[256,512]{1,0:T(8,128)(2,1)}, bf16[256,512]{1,0:T(8,128)(2,1)S(1)}, bf16[256,512]{1,0:T(8,128)(2,1)}) custom-call(bf16[4,256,512]{2,1,0:T(8,128)(2,1)} %get-tuple-element.44.refs_0_, bf16[4,256,512]{2,1,0:T(8,128)(2,1)} %collective-permute-done.4.refs_1_, bf16[4,256,512]{2,1,0:T(8,128)(2,1)} %collective-permute-done.5.refs_2_), custom_call_target="tpu_custom_call" | custom-call | bytes 1048576 | tf_op jit(solution)/shard_map/fold/pallas_call | solution.py:343
  61.6 2.2 %fold.3 = (bf16[256,512]{1,0:T(8,128)(2,1)S(1)}, bf16[256,512]{1,0:T(8,128)(2,1)}, bf16[256,512]{1,0:T(8,128)(2,1)}, bf16[256,512]{1,0:T(8,128)(2,1)}) custom-call(bf16[4,256,512]{2,1,0:T(8,128)(2,1)} %get-tuple-element.56.refs_0_, bf16[4,256,512]{2,1,0:T(8,128)(2,1)S(1)} %collective-permute-done.2.refs_1_, ...), custom_call_target="tpu_custom_call" | custom-call | bytes 1048576 | tf_op jit(solution)/shard_map/fold/pallas_call | solution.py:343
  63.9 1.3 collective-permute-start.10
  65.2 0.5 collective-permute-start.7
  65.7 2.2 %collective-permute-start.8 = (bf16[256,512]{1,0:T(8,128)(2,1)}, bf16[256,512]{1,0:T(8,128)(2,1)S(1)}, u32[]{:S(2)}, u32[]{:S(2)}) collective-permute-start(bf16[256,512]{1,0:T(8,128)(2,1)} %get-tuple-element.55), channel_id=1, source_target_pairs={{0,48},{16,0},{32,16},{48,32},{64,112},{80,64},{96,80},{112,96},{1... | collective-permute-start | bytes 786440 | tf_op jit(solution)/shard_map/ppermute | solution.py:392
  67.8 1.4 collective-permute-start.11
  69.3 4.1 %collective-permute-start.9 = (bf16[256,512]{1,0:T(8,128)(2,1)}, bf16[256,512]{1,0:T(8,128)(2,1)S(1)}, u32[]{:S(2)}, u32[]{:S(2)}) collective-permute-start(bf16[256,512]{1,0:T(8,128)(2,1)} %get-tuple-element.60), channel_id=1, source_target_pairs={{0,128},{16,144},{32,160},{48,176},{64,192},{80,208},{96,224},{112... | collective-permute-start | bytes 786440 | tf_op jit(solution)/shard_map/ppermute | solution.py:392
  73.4 0.6 dynamic_slice.3
  75.9 0.8 finish.2.refs_0_
  76.8 2.6 %collective-permute-done.9.refs_2_ = bf16[256,512]{1,0:T(8,128)(2,1)S(1)} collective-permute-done((bf16[256,512]{1,0:T(8,128)(2,1)}, bf16[256,512]{1,0:T(8,128)(2,1)S(1)}, u32[]{:S(2)}, u32[]{:S(2)}) %collective-permute-start.9) | collective-permute-done | bytes 262176 | tf_op jit(solution)/shard_map/ppermute | solution.py:392
  79.4 0.8 finish.3.grad
  80.4 11.5 %all-to-all-start.2 = ((bf16[16,32,512]{2,1,0:T(8,128)(2,1)}), bf16[16,32,512]{2,1,0:T(8,128)(2,1)S(1)}, u32[]{:S(2)}, u32[]{:S(2)}) async-start(bf16[16,32,512]{2,1,0:T(8,128)(2,1)} %bitcast.9), calls=%async_computation.2 | async-start | bytes 1048576 | tf_op jit(solution)/shard_map/all_to_all | solution.py:419
  92.0 17.2 %all-to-all-done.2.src = bf16[16,32,512]{2,1,0:T(8,128)(2,1)S(1)} async-done(((bf16[16,32,512]{2,1,0:T(8,128)(2,1)}), bf16[16,32,512]{2,1,0:T(8,128)(2,1)S(1)}, u32[]{:S(2)}, u32[]{:S(2)}) %all-to-all-start.2) | async-done | bytes 524320 | tf_op jit(solution)/shard_map/all_to_all | solution.py:419
  109.2 1.9 %pick.1 = bf16[32,32,512]{2,1,0:T(8,128)(2,1)} custom-call(s32[32]{0:T(128)S(1)} %broadcast_add_fusion.index, bf16[16,32,512]{2,1,0:T(8,128)(2,1)S(1)} %all-to-all-done.2.src), custom_call_target="tpu_custom_call" | custom-call | bytes 1048576 | tf_op jit(solution)/shard_map/pick/pallas_call | solution.py:236
  111.1 3.6 %all-to-all-start.3 = ((bf16[16,2,32,512]{3,2,1,0:T(8,128)(2,1)}), bf16[16,2,32,512]{3,2,1,0:T(8,128)(2,1)S(1)}, u32[]{:S(2)}, u32[]{:S(2)}) async-start(bf16[16,2,32,512]{3,2,1,0:T(8,128)(2,1)} %bitcast.10), calls=%async_computation.3 | async-start | bytes 2097152 | tf_op jit(solution)/shard_map/all_to_all | solution.py:421
  114.7 2.7 %precondition.1 = bf16[512,512]{1,0:T(8,128)(2,1)} custom-call(bf16[2,512,512]{2,1,0:T(8,128)(2,1)S(1)} %unpack_roots.1.roots, bf16[512,512]{1,0:T(8,128)(2,1)} %finish.3.grad), custom_call_target="tpu_custom_call" | custom-call | flops 536870912 | bytes 2097152 | tf_op jit(solution)/shard_map/precondition/pallas_call | solution.py:298
  117.4 24.6 %all-to-all-done.3.grads = bf16[16,2,32,512]{3,2,1,0:T(8,128)(2,1)S(1)} async-done(((bf16[16,2,32,512]{3,2,1,0:T(8,128)(2,1)}), bf16[16,2,32,512]{3,2,1,0:T(8,128)(2,1)S(1)}, u32[]{:S(2)}, u32[]{:S(2)}) %all-to-all-start.3) | async-done | bytes 1048608 | tf_op jit(solution)/shard_map/all_to_all | solution.py:421
  142.0 3.4 %grams.1 = (bf16[2,512,512]{2,1,0:T(8,128)(2,1)}, bf16[2,512,512]{2,1,0:T(8,128)(2,1)}) custom-call(bf16[16,2,32,512]{3,2,1,0:T(8,128)(2,1)S(1)} %all-to-all-done.3.grads, bf16[2,512,512]{2,1,0:T(8,128)(2,1)S(1)} %bitcast.22, bf16[2,512,512]{2,1,0:T(8,128)(2,1)} %bitcast.24), custom_call_target="tpu_custom_call" | custom-call | flops 1073741824 | bytes 5242880 | tf_op jit(solution)/shard_map/grams/pallas_call | solution.py:319
  (30 shorter events, 1.1 us)
Async XLA Ops:
  0.7 11.6 %copy-start = (bf16[1,1,2,512,512]{4,3,2,1,0:T(8,128)(2,1)S(1)}, bf16[1,1,2,512,512]{4,3,2,1,0:T(8,128)(2,1)}, u32[]{:S(2)}) copy-start(bf16[1,1,2,512,512]{4,3,2,1,0:T(8,128)(2,1)} %param.12) | copy-start | bytes 3145732
  0.7 11.6 %copy-start.1 = (bf16[1,1,2,512,512]{4,3,2,1,0:T(8,128)(2,1)S(1)}, bf16[1,1,2,512,512]{4,3,2,1,0:T(8,128)(2,1)}, u32[]{:S(2)}) copy-start(bf16[1,1,2,512,512]{4,3,2,1,0:T(8,128)(2,1)} %param.13) | copy-start | bytes 3145732
  5.7 27.9 %collective-permute-start = (bf16[4,256,512]{2,1,0:T(8,128)(2,1)}, bf16[4,256,512]{2,1,0:T(8,128)(2,1)}, u32[]{:S(2)}, u32[]{:S(2)}) collective-permute-start(bf16[4,256,512]{2,1,0:T(8,128)(2,1)} %get-tuple-element.37), channel_id=1, source_target_pairs={{0,32},{16,48},{32,0},{48,16},{64,96},{80,112},{96,64},{112,80},{1... | collective-permute-start | bytes 3145736 | tf_op jit(solution)/shard_map/ppermute | solution.py:392
  9.4 26.7 %collective-permute-start.1 = (bf16[4,256,512]{2,1,0:T(8,128)(2,1)}, bf16[4,256,512]{2,1,0:T(8,128)(2,1)}, u32[]{:S(2)}, u32[]{:S(2)}) collective-permute-start(bf16[4,256,512]{2,1,0:T(8,128)(2,1)} %get-tuple-element.41), channel_id=1, source_target_pairs={{0,128},{16,144},{32,160},{48,176},{64,192},{80,208},{96,224},{112... | collective-permute-start | bytes 3145736 | tf_op jit(solution)/shard_map/ppermute | solution.py:392
  13.6 39.1 %all-to-all-start = ((bf16[16,272,128]{2,1,0:T(8,128)(2,1)}), bf16[16,272,128]{2,1,0:T(8,128)(2,1)}, u32[]{:S(2)}, u32[]{:S(2)}) async-start(bf16[16,272,128]{2,1,0:T(8,128)(2,1)} %pack_roots.1), calls=%async_computation | async-start | bytes 2228224 | tf_op jit(solution)/shard_map/all_to_all | solution.py:396
  23.3 12.6 %copy-start.3 = (s32[1,16]{1,0:T(1,128)S(1)}, s32[1,16]{1,0:T(1,128)}, u32[]{:S(2)}) copy-start(s32[1,16]{1,0:T(1,128)} %param.9) | copy-start | bytes 196
  30.5 27.9 %collective-permute-start.2 = (bf16[4,256,512]{2,1,0:T(8,128)(2,1)}, bf16[4,256,512]{2,1,0:T(8,128)(2,1)S(1)}, u32[]{:S(2)}, u32[]{:S(2)}) collective-permute-start(bf16[4,256,512]{2,1,0:T(8,128)(2,1)} %get-tuple-element.45), channel_id=1, source_target_pairs={{0,16},{16,32},{32,48},{48,0},{64,80},{80,96},{96,112},{112,64},{1... | collective-permute-start | bytes 3145736 | tf_op jit(solution)/shard_map/ppermute | solution.py:392
  30.9 27.5 %collective-permute-start.3 = (bf16[4,256,512]{2,1,0:T(8,128)(2,1)}, bf16[4,256,512]{2,1,0:T(8,128)(2,1)S(1)}, u32[]{:S(2)}, u32[]{:S(2)}) collective-permute-start(bf16[4,256,512]{2,1,0:T(8,128)(2,1)} %get-tuple-element.46), channel_id=1, source_target_pairs={{0,48},{16,0},{32,16},{48,32},{64,112},{80,64},{96,80},{112,96},{1... | collective-permute-start | bytes 3145736 | tf_op jit(solution)/shard_map/ppermute | solution.py:392
  33.2 25.5 %collective-permute-start.4 = (bf16[4,256,512]{2,1,0:T(8,128)(2,1)}, bf16[4,256,512]{2,1,0:T(8,128)(2,1)}, u32[]{:S(2)}, u32[]{:S(2)}) collective-permute-start(bf16[4,256,512]{2,1,0:T(8,128)(2,1)} %get-tuple-element.47), channel_id=1, source_target_pairs={{0,64},{16,80},{32,96},{48,112},{64,128},{80,144},{96,160},{112,17... | collective-permute-start | bytes 3145736 | tf_op jit(solution)/shard_map/ppermute | solution.py:392
  33.6 25.1 %collective-permute-start.5 = (bf16[4,256,512]{2,1,0:T(8,128)(2,1)}, bf16[4,256,512]{2,1,0:T(8,128)(2,1)}, u32[]{:S(2)}, u32[]{:S(2)}) collective-permute-start(bf16[4,256,512]{2,1,0:T(8,128)(2,1)} %get-tuple-element.48), channel_id=1, source_target_pairs={{0,192},{16,208},{32,224},{48,240},{64,0},{80,16},{96,32},{112,48}... | collective-permute-start | bytes 3145736 | tf_op jit(solution)/shard_map/ppermute | solution.py:392
  54.8 25.4 %all-to-all-start.1 = ((bf16[16,144,128]{2,1,0:T(8,128)(2,1)}), bf16[16,144,128]{2,1,0:T(8,128)(2,1)S(1)}, u32[]{:S(2)}, u32[]{:S(2)}) async-start(bf16[16,144,128]{2,1,0:T(8,128)(2,1)} %pick_roots.1), calls=%async_computation.1 | async-start | bytes 1179648 | tf_op jit(solution)/shard_map/all_to_all | solution.py:411
  61.5 7.8 %collective-permute-start.6 = (bf16[256,512]{1,0:T(8,128)(2,1)S(1)}, bf16[256,512]{1,0:T(8,128)(2,1)S(1)}, u32[]{:S(2)}, u32[]{:S(2)}) collective-permute-start(bf16[256,512]{1,0:T(8,128)(2,1)S(1)} %get-tuple-element.53), channel_id=1, source_target_pairs={{0,32},{16,48},{32,0},{48,16},{64,96},{80,112},{96,64},{112,80},{1... | collective-permute-start | bytes 786440 | tf_op jit(solution)/shard_map/ppermute | solution.py:392
  63.9 12.9 %collective-permute-start.10 = (bf16[256,512]{1,0:T(8,128)(2,1)}, bf16[256,512]{1,0:T(8,128)(2,1)S(1)}, u32[]{:S(2)}, u32[]{:S(2)}) collective-permute-start(bf16[256,512]{1,0:T(8,128)(2,1)} %get-tuple-element.61), channel_id=1, source_target_pairs={{0,64},{16,80},{32,96},{48,112},{64,128},{80,144},{96,160},{112,17... | collective-permute-start | bytes 786440 | tf_op jit(solution)/shard_map/ppermute | solution.py:392
  65.2 10.8 %collective-permute-start.7 = (bf16[256,512]{1,0:T(8,128)(2,1)}, bf16[256,512]{1,0:T(8,128)(2,1)S(1)}, u32[]{:S(2)}, u32[]{:S(2)}) collective-permute-start(bf16[256,512]{1,0:T(8,128)(2,1)} %get-tuple-element.54), channel_id=1, source_target_pairs={{0,16},{16,32},{32,48},{48,0},{64,80},{80,96},{96,112},{112,64},{1... | collective-permute-start | bytes 786440 | tf_op jit(solution)/shard_map/ppermute | solution.py:392
  65.7 10.3 %collective-permute-start.8 = (bf16[256,512]{1,0:T(8,128)(2,1)}, bf16[256,512]{1,0:T(8,128)(2,1)S(1)}, u32[]{:S(2)}, u32[]{:S(2)}) collective-permute-start(bf16[256,512]{1,0:T(8,128)(2,1)} %get-tuple-element.55), channel_id=1, source_target_pairs={{0,48},{16,0},{32,16},{48,32},{64,112},{80,64},{96,80},{112,96},{1... | collective-permute-start | bytes 786440 | tf_op jit(solution)/shard_map/ppermute | solution.py:392
  67.8 8.9 %collective-permute-start.11 = (bf16[256,512]{1,0:T(8,128)(2,1)}, bf16[256,512]{1,0:T(8,128)(2,1)S(1)}, u32[]{:S(2)}, u32[]{:S(2)}) collective-permute-start(bf16[256,512]{1,0:T(8,128)(2,1)} %get-tuple-element.62), channel_id=1, source_target_pairs={{0,192},{16,208},{32,224},{48,240},{64,0},{80,16},{96,32},{112,48}... | collective-permute-start | bytes 786440 | tf_op jit(solution)/shard_map/ppermute | solution.py:392
  69.3 10.1 %collective-permute-start.9 = (bf16[256,512]{1,0:T(8,128)(2,1)}, bf16[256,512]{1,0:T(8,128)(2,1)S(1)}, u32[]{:S(2)}, u32[]{:S(2)}) collective-permute-start(bf16[256,512]{1,0:T(8,128)(2,1)} %get-tuple-element.60), channel_id=1, source_target_pairs={{0,128},{16,144},{32,160},{48,176},{64,192},{80,208},{96,224},{112... | collective-permute-start | bytes 786440 | tf_op jit(solution)/shard_map/ppermute | solution.py:392
  80.4 28.8 %all-to-all-start.2 = ((bf16[16,32,512]{2,1,0:T(8,128)(2,1)}), bf16[16,32,512]{2,1,0:T(8,128)(2,1)S(1)}, u32[]{:S(2)}, u32[]{:S(2)}) async-start(bf16[16,32,512]{2,1,0:T(8,128)(2,1)} %bitcast.9), calls=%async_computation.2 | async-start | bytes 1048576 | tf_op jit(solution)/shard_map/all_to_all | solution.py:419
  111.1 30.8 %all-to-all-start.3 = ((bf16[16,2,32,512]{3,2,1,0:T(8,128)(2,1)}), bf16[16,2,32,512]{3,2,1,0:T(8,128)(2,1)S(1)}, u32[]{:S(2)}, u32[]{:S(2)}) async-start(bf16[16,2,32,512]{3,2,1,0:T(8,128)(2,1)} %bitcast.10), calls=%async_computation.3 | async-start | bytes 2097152 | tf_op jit(solution)/shard_map/all_to_all | solution.py:421
  114.7 27.3 %copy-start.2 = (bf16[1,1,2,512,512]{4,3,2,1,0:T(8,128)(2,1)S(1)}, bf16[1,1,2,512,512]{4,3,2,1,0:T(8,128)(2,1)}, u32[]{:S(2)}) copy-start(bf16[1,1,2,512,512]{4,3,2,1,0:T(8,128)(2,1)} %param.10) | copy-start | bytes 3145732
